TPU v7x, 32 devices: a whole 2x2x4 slice. The times are simulated.
32 devices in a mesh: leaf: 32 (over z, y, x, core).
Axes of the slice: x: 2, y: 2, z: 4, core: 2. Of those that a mesh axis runs over, the one named last changes fastest.
Arguments:
- right_hand: float32 [512, 32, 256], P('leaf')
- leaf_live: int32 [512], P('leaf'), may hold values from 0 to 1, as said below
- near_index: int32 [512, 6], P('leaf'), may hold values from 0 to 511, as said below
- near_tile: bfloat16 [512, 6, 256, 256], P('leaf'), may hold values from -1 to 5
- far_index: int32 [512, 8], P('leaf'), may hold values from 0 to 511, as said below
- far_couple: bfloat16 [512, 8, 64, 64], P('leaf'), may hold values from -0.25 to 0.25
- leaf_basis: bfloat16 [512, 64, 256], P('leaf'), may hold values from -0.375 to 0.375
- leaf_transfer: bfloat16 [512, 64, 64], P('leaf'), may hold values from -0.1875 to 0.1875
- tree_up: bfloat16 [62, 64, 64], replicated, may hold values from -0.5 to 0.5
- tree_couple: bfloat16 [62, 64, 64], replicated, may hold values from -0.75 to 0.75
Outputs:
- basis_next: float32 [512, 32, 256], P('leaf')
- hessenberg: float32 [6, 32], replicated
Inputs may be any that keep to these rules, and one draw needn't show every extreme that they name: `leaf_live`: each device's 16 slots hold between 5 and 16 live leaves, both counts reached on some device; which slots are live is arbitrary. `near_index`: entry 0 of each row is the row's own slot; every entry lies within 2 slots of its row's slot, and some entry lies exactly 2 away; entries may name dead slots. `far_index`: every entry lies within 16 slots of its row's slot, and some entry lies exactly 16 away; entries may name dead slots.
All inputs are finite; a program needn't handle non-finite values.
Results may differ from a plain program's by a relative error of at most 0.009.
Values may be sent and summed in bfloat16 or wider, within the bound.
A program may use at most 128 MiB of HBM per device.

v0:
```python
import jax
import jax.numpy as jnp
from jax import lax
from jax.sharding import PartitionSpec as P

epsilon = 1e-06


def with_halo(array, sides, width):
    for axis, dim in sides:
        size, length = (lax.axis_size(axis), array.shape[dim])
        up = [(i, (i + 1) % size) for i in range(size - 1)]
        down = [(j, i) for i, j in up]
        last = lax.slice_in_dim(array, length - width, length, axis=dim)
        initial = lax.slice_in_dim(array, 0, width, axis=dim)
        before = lax.ppermute(last, axis, up)
        after = lax.ppermute(initial, axis, down)
        array = jnp.concatenate([before, array, after], axis=dim)
    return array


def swapped(array, axis, stride):
    return lax.ppermute(array, axis, [(i, i ^ 1 << stride) for i in range(lax.axis_size(axis))])


def apply_operator(
    vector,
    leaf_live,
    near_index,
    near_tile,
    far_index,
    far_couple,
    leaf_basis,
    leaf_transfer,
    tree_up,
    tree_couple,
):
    position = lax.axis_index("leaf")
    device_total = lax.axis_size("leaf")
    slot_count = vector.shape[0]
    live_mask = leaf_live.astype(jnp.float32)[:, None, None]
    inputs = (vector * live_mask).astype(jnp.bfloat16)
    padded = with_halo(inputs, (("leaf", 0),), slot_count)
    local_near = near_index - (position * slot_count - slot_count)
    columns = padded[local_near]
    near = jnp.einsum("inrp,inpq->irq", columns, near_tile, preferred_element_type=jnp.float32)
    moments = jnp.einsum(
        "irp,ikp->irk", inputs, leaf_basis, preferred_element_type=jnp.float32
    ).astype(jnp.bfloat16)
    moment_pad = with_halo(moments, (("leaf", 0),), slot_count)
    local_far = far_index - (position * slot_count - slot_count)
    far_term = jnp.einsum(
        "ifrk,ifkj->irj", moment_pad[local_far], far_couple, preferred_element_type=jnp.float32
    )
    box_moment = jnp.einsum(
        "irk,ikj->rj", moments, leaf_transfer, preferred_element_type=jnp.float32
    ).astype(jnp.bfloat16)
    levels = device_total.bit_length() - 1
    locals_list = []
    current = box_moment
    for level in range(levels):
        level_first = 2 * device_total - 2 * (device_total >> level)
        own_node = level_first + (position >> level)
        other_node = level_first + (position >> level ^ 1)
        sibling = swapped(current, "leaf", level)
        locals_list.append(
            jnp.dot(sibling, tree_couple[own_node], preferred_element_type=jnp.float32)
        )
        lifted = jnp.dot(current, tree_up[own_node], preferred_element_type=jnp.float32) + jnp.dot(
            sibling, tree_up[other_node], preferred_element_type=jnp.float32
        )
        current = lifted.astype(jnp.bfloat16)
    downward = jnp.zeros(box_moment.shape, jnp.bfloat16)
    for level in reversed(range(levels)):
        level_first = 2 * device_total - 2 * (device_total >> level)
        own_node = level_first + (position >> level)
        carried = jnp.einsum(
            "rj,kj->rk", downward, tree_up[own_node], preferred_element_type=jnp.float32
        )
        downward = (locals_list[level] + carried).astype(jnp.bfloat16)
    leaf_down = jnp.einsum(
        "rj,ikj->irk", downward, leaf_transfer, preferred_element_type=jnp.float32
    )
    local_total = (far_term + leaf_down).astype(jnp.bfloat16)
    spread = jnp.einsum("irk,ikp->irp", local_total, leaf_basis, preferred_element_type=jnp.float32)
    return live_mask * (near + spread)


def column_sums(first_field, second_field):
    return jnp.sum(first_field * second_field, axis=(0, 2))


def global_norm(field):
    return jnp.sqrt(lax.psum(column_sums(field, field), "leaf") + epsilon)


def joint_totals(stacked):
    return lax.psum(stacked, "leaf")


def on_device(
    right_hand,
    leaf_live,
    near_index,
    near_tile,
    far_index,
    far_couple,
    leaf_basis,
    leaf_transfer,
    tree_up,
    tree_couple,
):

    def operator(vector):
        return apply_operator(
            vector,
            leaf_live,
            near_index,
            near_tile,
            far_index,
            far_couple,
            leaf_basis,
            leaf_transfer,
            tree_up,
            tree_couple,
        )

    live_mask = leaf_live.astype(jnp.float32)[:, None, None]
    start_vec = right_hand * live_mask
    norm_start = global_norm(start_vec)
    basis_one = start_vec / norm_start[None, :, None]
    image_one = operator(basis_one)
    first_set = joint_totals(
        jnp.stack(
            [
                column_sums(basis_one, image_one),
                column_sums(image_one, image_one),
                column_sums(basis_one, basis_one),
            ]
        )
    )
    first_inner = first_set[0]
    first_square = (
        first_set[1] - 2.0 * first_inner * first_inner + first_inner * first_inner * first_set[2]
    )
    first_length = jnp.sqrt(first_square + epsilon)
    residue_one = image_one - first_inner[None, :, None] * basis_one
    basis_two = residue_one / first_length[None, :, None]
    image_two = operator(basis_two)
    second_set = joint_totals(
        jnp.stack(
            [
                column_sums(basis_one, image_two),
                column_sums(basis_two, image_two),
                column_sums(image_two, image_two),
                column_sums(basis_one, basis_one),
                column_sums(basis_two, basis_two),
                column_sums(basis_one, basis_two),
            ]
        )
    )
    cross_inner = second_set[0]
    self_inner = second_set[1]
    second_square = (
        second_set[2]
        - 2.0 * cross_inner * cross_inner
        - 2.0 * self_inner * self_inner
        + cross_inner * cross_inner * second_set[3]
        + self_inner * self_inner * second_set[4]
        + 2.0 * cross_inner * self_inner * second_set[5]
    )
    second_length = jnp.sqrt(second_square + epsilon)
    residue_two = (
        image_two - cross_inner[None, :, None] * basis_one - self_inner[None, :, None] * basis_two
    )
    basis_next = residue_two / second_length[None, :, None]
    hessenberg = jnp.stack(
        [norm_start, first_inner, first_length, cross_inner, self_inner, second_length]
    )
    return (basis_next, hessenberg)


def solution(mesh):
    placed = (
        P("leaf", None, None),
        P("leaf"),
        P("leaf", None),
        P("leaf", None, None, None),
        P("leaf", None),
        P("leaf", None, None, None),
        P("leaf", None, None),
        P("leaf", None, None),
        P(),
        P(),
    )
    return jax.shard_map(
        on_device,
        mesh=mesh,
        in_specs=placed,
        out_specs=(P("leaf", None, None), P()),
        check_vma=False,
    )
```

profile of v0, /device:TPU:0, one launch (start us, length us, event | category | flops | bytes accessed | tf_op | source)
XLA Modules:
  0.0 250.6 jit_solution(13067751719531946111)
XLA Ops:
  1.5 1.3 multiply_reduce_fusion.8
  2.8 42.0 %psum.21 = f32[32]{0:T(128)S(1)} all-reduce(f32[32]{0:T(128)S(1)} %multiply_reduce_fusion.8), channel_id=1, replica_groups=mesh['leaf'=32] {'leaf'}, use_global_device_ids=true, to_apply=%region_1.0 | all-reduce | flops 32 | bytes 256 | tf_op jit(solution)/shard_map/psum | solution.py:94
  45.3 1.9 multiply_convert_fusion.1
  47.2 1.4 convolution_convert_fusion.1
  48.6 1.3 collective-permute-start.3
  49.9 3.7 %collective-permute-start.2 = (bf16[16,32,64]{2,1,0:T(8,128)(2,1)S(1)}, bf16[16,32,64]{2,1,0:T(8,128)(2,1)}, u32[]{:S(2)}, u32[]{:S(2)}) collective-permute-start(bf16[16,32,64]{2,1,0:T(8,128)(2,1)S(1)} %convolution_convert_fusion.1), channel_id=1, source_target_pairs={{0,1},{1,2},{2,3},{3,4},{4,5},{5,6},{6,7},{7,8},{8,9},{9,10},{10,1... | collective-permute-start | bytes 196616 | tf_op jit(solution)/shard_map/ppermute | solution.py:16
  53.6 1.3 collective-permute-start.1
  54.9 4.5 %collective-permute-start = (bf16[16,32,256]{2,1,0:T(8,128)(2,1)}, bf16[16,32,256]{2,1,0:T(8,128)(2,1)}, u32[]{:S(2)}, u32[]{:S(2)}) collective-permute-start(bf16[16,32,256]{2,1,0:T(8,128)(2,1)} %get-tuple-element.12), channel_id=1, source_target_pairs={{0,1},{1,2},{2,3},{3,4},{4,5},{5,6},{6,7},{7,8},{8,9},{9,10},{10,1... | collective-permute-start | bytes 786440 | tf_op jit(solution)/shard_map/ppermute | solution.py:16
  59.6 1.1 collective-permute-start.4
  64.2 2.4 collective-permute-start.5
  69.1 2.5 collective-permute-start.6
  74.0 1.5 collective-permute-start.7
  76.3 1.3 collective-permute-done.7
  78.5 2.3 collective-permute-start.8
  81.4 1.6 collective-permute-done.8
  84.0 1.0 fusion.36
  85.0 1.0 fusion.37
  86.0 1.0 fusion.38
  86.9 1.4 fusion.39
  88.4 1.0 pad_maximum_fusion.2
  89.4 1.8 gather_fusion.1
  91.2 2.4 convolution_bitcast_fusion.5
  93.6 2.2 fusion.9
  95.9 2.1 pad_maximum_fusion
  97.9 3.0 %gather_fusion = bf16[96,32,256]{2,1,0:T(8,128)(2,1)} fusion(bf16[48,32,256]{2,1,0:T(8,128)(2,1)} %pad_maximum_fusion, s32[1024]{0:T(1024)S(1)} %copy-done.7), kind=kCustom, calls=%fused_computation | custom fusion | bytes 3146112 | tf_op jit(solution)/shard_map/gather | solution.py:45
  101.0 8.2 %multiply_reduce_fusion.7 = (f32[32]{0:T(128)S(1)}, f32[32]{0:T(128)S(1)}, f32[32]{0:T(128)S(1)}, f32[16,32,256]{2,1,0:T(8,128)}) fusion(f32[16,32,256]{2,1,0:T(8,128)S(1)} %get-tuple-element.13, f32[16,32,256]{2,1,0:T(8,128)} %fusion.9, bf16[16,6,32,256]{3,2,1,0:T(8,128)(2,1)} %bitcast.250, bf16[16,6,256,256]{3,2,1,0:T(8,128)(2,1)} %param.13, ...), kind=kOutput, calls=%fused_computation.84 | convolution fusion | flops 403701664 | bytes 15729088 | tf_op jit(solution)/shard_map/inrp,inpq->irq/dot_general | solution.py:46
  109.7 41.3 %psum.22 = f32[3,32]{1,0:T(4,128)S(1)} all-reduce(f32[3,32]{1,0:T(4,128)S(1)} %pad_maximum_fusion.4), channel_id=1, replica_groups=mesh['leaf'=32] {'leaf'}, use_global_device_ids=true, to_apply=%region_5.0 | all-reduce | flops 96 | bytes 768 | tf_op jit(solution)/shard_map/psum | solution.py:98
  151.5 2.1 multiply_convert_fusion
  153.6 1.2 convolution_convert_fusion
  157.1 2.3 collective-permute-start.14
  161.8 2.0 collective-permute-start.15
  167.7 2.3 collective-permute-done.16
  171.6 1.3 collective-permute-start.12
  172.9 3.7 %collective-permute-start.11 = (bf16[16,32,64]{2,1,0:T(8,128)(2,1)S(1)}, bf16[16,32,64]{2,1,0:T(8,128)(2,1)}, u32[]{:S(2)}, u32[]{:S(2)}) collective-permute-start(bf16[16,32,64]{2,1,0:T(8,128)(2,1)S(1)} %convolution_convert_fusion), channel_id=1, source_target_pairs={{0,1},{1,2},{2,3},{3,4},{4,5},{5,6},{6,7},{7,8},{8,9},{9,10},{10,1... | collective-permute-start | bytes 196616 | tf_op jit(solution)/shard_map/ppermute | solution.py:16
  176.6 1.3 collective-permute-start.10
  177.9 4.3 %collective-permute-start.9 = (bf16[16,32,256]{2,1,0:T(8,128)(2,1)}, bf16[16,32,256]{2,1,0:T(8,128)(2,1)}, u32[]{:S(2)}, u32[]{:S(2)}) collective-permute-start(bf16[16,32,256]{2,1,0:T(8,128)(2,1)} %get-tuple-element.10), channel_id=1, source_target_pairs={{0,1},{1,2},{2,3},{3,4},{4,5},{5,6},{6,7},{7,8},{8,9},{9,10},{10,1... | collective-permute-start | bytes 786440 | tf_op jit(solution)/shard_map/ppermute | solution.py:16
  183.1 1.0 fusion.31
  184.1 1.0 fusion.32
  185.1 1.0 fusion.33
  187.5 1.1 pad_maximum_fusion.3
  188.7 1.8 gather_fusion.3
  190.4 2.4 convolution_bitcast_fusion.3
  192.9 2.2 fusion.8
  195.1 1.2 pad_maximum_fusion.1
  196.3 1.9 gather_fusion.2
  198.2 8.4 %multiply_reduce_fusion = (f32[32]{0:T(128)S(1)}, f32[32]{0:T(128)S(1)}, f32[32]{0:T(128)S(1)}, f32[32]{0:T(128)S(1)}, f32[32]{0:T(128)S(1)}, /*index=5*/f32[16,32,256]{2,1,0:T(8,128)}) fusion(f32[16,32,256]{2,1,0:T(8,128)S(1)} %get-tuple-element.13, f32[16,32,256]{2,1,0:T(8,128)} %get-tuple-element.11, f32[16,32,256]{2,1,0:T(8,128)} %fusion.8, ...), kind=kOutput, calls=%fused_computation.75 | convolution fusion | flops 404225888 | bytes 16253632 | tf_op jit(solution)/shard_map/inrp,inpq->irq/dot_general | solution.py:46
  206.7 41.2 %psum.23 = f32[6,32]{1,0:T(8,128)S(1)} all-reduce(f32[6,32]{1,0:T(8,128)S(1)} %stack.49), channel_id=1, replica_groups=mesh['leaf'=32] {'leaf'}, use_global_device_ids=true, to_apply=%region_11.0 | all-reduce | flops 192 | bytes 1536 | tf_op jit(solution)/shard_map/psum | solution.py:98
  247.9 2.0 subtract_divide_fusion
  (98 shorter events, 27.8 us)
Async XLA Ops:
  0.6 90.5 %copy-start = (bf16[16,8,64,64]{3,2,1,0:T(8,128)(2,1)S(1)}, bf16[16,8,64,64]{3,2,1,0:T(8,128)(2,1)}, u32[]{:S(2)}) copy-start(bf16[16,8,64,64]{3,2,1,0:T(8,128)(2,1)} %param.15) | copy-start | bytes 3145732
  0.6 58.7 %copy-start.3 = (bf16[16,64,64]{2,1,0:T(8,128)(2,1)S(1)}, bf16[16,64,64]{2,1,0:T(8,128)(2,1)}, u32[]{:S(2)}) copy-start(bf16[16,64,64]{2,1,0:T(8,128)(2,1)} %param.17) | copy-start | bytes 393220
  0.7 60.0 %copy-start.15 = (s32[16,6]{0,1:T(8,128)S(1)}, s32[16,6]{0,1:T(8,128)}, u32[]{:S(2)}) copy-start(s32[16,6]{0,1:T(8,128)} %param.12) | copy-start | bytes 1156
  0.7 60.0 %copy-start.16 = (s32[16,8]{0,1:T(8,128)S(1)}, s32[16,8]{0,1:T(8,128)}, u32[]{:S(2)}) copy-start(s32[16,8]{0,1:T(8,128)} %param.14) | copy-start | bytes 1540
  1.5 59.4 %copy-start.9 = (f32[16]{0:T(128)}, f32[16]{0:T(128)S(1)}, u32[]{:S(2)}) copy-start(f32[16]{0:T(128)S(1)} %convert_element_type.83) | copy-start | bytes 196
  48.6 39.8 %collective-permute-start.3 = (bf16[16,32,64]{2,1,0:T(8,128)(2,1)S(1)}, bf16[16,32,64]{2,1,0:T(8,128)(2,1)S(1)}, u32[]{:S(2)}, u32[]{:S(2)}) collective-permute-start(bf16[16,32,64]{2,1,0:T(8,128)(2,1)S(1)} %convolution_convert_fusion.1), channel_id=1, source_target_pairs={{1,0},{2,1},{3,2},{4,3},{5,4},{6,5},{7,6},{8,7},{9,8},{10,9},{11,1... | collective-permute-start | bytes 196616 | tf_op jit(solution)/shard_map/ppermute | solution.py:17
  49.9 38.5 %collective-permute-start.2 = (bf16[16,32,64]{2,1,0:T(8,128)(2,1)S(1)}, bf16[16,32,64]{2,1,0:T(8,128)(2,1)}, u32[]{:S(2)}, u32[]{:S(2)}) collective-permute-start(bf16[16,32,64]{2,1,0:T(8,128)(2,1)S(1)} %convolution_convert_fusion.1), channel_id=1, source_target_pairs={{0,1},{1,2},{2,3},{3,4},{4,5},{5,6},{6,7},{7,8},{8,9},{9,10},{10,1... | collective-permute-start | bytes 196616 | tf_op jit(solution)/shard_map/ppermute | solution.py:16
  53.6 42.3 %collective-permute-start.1 = (bf16[16,32,256]{2,1,0:T(8,128)(2,1)}, bf16[16,32,256]{2,1,0:T(8,128)(2,1)}, u32[]{:S(2)}, u32[]{:S(2)}) collective-permute-start(bf16[16,32,256]{2,1,0:T(8,128)(2,1)} %get-tuple-element.12), channel_id=1, source_target_pairs={{1,0},{2,1},{3,2},{4,3},{5,4},{6,5},{7,6},{8,7},{9,8},{10,9},{11,1... | collective-permute-start | bytes 786440 | tf_op jit(solution)/shard_map/ppermute | solution.py:17
  54.9 41.0 %collective-permute-start = (bf16[16,32,256]{2,1,0:T(8,128)(2,1)}, bf16[16,32,256]{2,1,0:T(8,128)(2,1)}, u32[]{:S(2)}, u32[]{:S(2)}) collective-permute-start(bf16[16,32,256]{2,1,0:T(8,128)(2,1)} %get-tuple-element.12), channel_id=1, source_target_pairs={{0,1},{1,2},{2,3},{3,4},{4,5},{5,6},{6,7},{7,8},{8,9},{9,10},{10,1... | collective-permute-start | bytes 786440 | tf_op jit(solution)/shard_map/ppermute | solution.py:16
  59.6 3.8 %collective-permute-start.4 = (bf16[32,64]{1,0:T(8,128)(2,1)S(1)}, bf16[32,64]{1,0:T(8,128)(2,1)S(1)}, u32[]{:S(2)}, u32[]{:S(2)}) collective-permute-start(bf16[32,64]{1,0:T(8,128)(2,1)S(1)} %fusion.10), channel_id=1, source_target_pairs={{0,1},{1,0},{2,3},{3,2},{4,5},{5,4},{6,7},{7,6},{8,9},{9,8},{10,11... | collective-permute-start | bytes 12296 | tf_op jit(solution)/shard_map/ppermute | solution.py:23
  64.2 4.0 %collective-permute-start.5 = (bf16[32,64]{1,0:T(8,128)(2,1)S(1)}, bf16[32,64]{1,0:T(8,128)(2,1)S(1)}, u32[]{:S(2)}, u32[]{:S(2)}) collective-permute-start(bf16[32,64]{1,0:T(8,128)(2,1)S(1)} %fusion.13), channel_id=1, source_target_pairs={{0,2},{1,3},{2,0},{3,1},{4,6},{5,7},{6,4},{7,5},{8,10},{9,11},{10,... | collective-permute-start | bytes 12296 | tf_op jit(solution)/shard_map/ppermute | solution.py:23
  69.1 4.1 %collective-permute-start.6 = (bf16[32,64]{1,0:T(8,128)(2,1)S(1)}, bf16[32,64]{1,0:T(8,128)(2,1)S(1)}, u32[]{:S(2)}, u32[]{:S(2)}) collective-permute-start(bf16[32,64]{1,0:T(8,128)(2,1)S(1)} %fusion.15), channel_id=1, source_target_pairs={{0,4},{1,5},{2,6},{3,7},{4,0},{5,1},{6,2},{7,3},{8,12},{9,13},{10,... | collective-permute-start | bytes 12296 | tf_op jit(solution)/shard_map/ppermute | solution.py:23
  74.0 3.7 %collective-permute-start.7 = (bf16[32,64]{1,0:T(8,128)(2,1)S(1)}, bf16[32,64]{1,0:T(8,128)(2,1)S(1)}, u32[]{:S(2)}, u32[]{:S(2)}) collective-permute-start(bf16[32,64]{1,0:T(8,128)(2,1)S(1)} %fusion.17), channel_id=1, source_target_pairs={{0,8},{1,9},{2,10},{3,11},{4,12},{5,13},{6,14},{7,15},{8,0},{9,1},... | collective-permute-start | bytes 12296 | tf_op jit(solution)/shard_map/ppermute | solution.py:23
  78.5 4.6 %collective-permute-start.8 = (bf16[32,64]{1,0:T(8,128)(2,1)S(1)}, bf16[32,64]{1,0:T(8,128)(2,1)S(1)}, u32[]{:S(2)}, u32[]{:S(2)}) collective-permute-start(bf16[32,64]{1,0:T(8,128)(2,1)S(1)} %fusion.19), channel_id=1, source_target_pairs={{0,16},{1,17},{2,18},{3,19},{4,20},{5,21},{6,22},{7,23},{8,24},{9,... | collective-permute-start | bytes 12296 | tf_op jit(solution)/shard_map/ppermute | solution.py:23
  91.2 2.5 copy-start.1
  91.2 2.5 copy-start.12
  93.6 4.3 %copy-start.7 = (s32[1024]{0:T(1024)S(1)}, s32[1024]{0:T(1024)}, u32[]{:S(2)}) copy-start(s32[1024]{0:T(1024)} %pad_clamp_fusion.1) | copy-start | bytes 12292
  95.8 5.1 %copy-start.10 = (f32[16]{0:T(128)S(1)}, f32[16]{0:T(128)}, u32[]{:S(2)}) copy-start(f32[16]{0:T(128)} %copy-done.9) | copy-start | bytes 196
  109.1 0.5 copy-start.13
  154.8 32.1 %copy-start.5 = (bf16[16,32,64]{2,1,0:T(8,128)(2,1)}, bf16[16,32,64]{2,1,0:T(8,128)(2,1)S(1)}, u32[]{:S(2)}) copy-start(bf16[16,32,64]{2,1,0:T(8,128)(2,1)S(1)} %convolution_convert_fusion) | copy-start | bytes 196612
  155.0 1.2 collective-permute-start.13
  157.1 3.9 %collective-permute-start.14 = (bf16[32,64]{1,0:T(8,128)(2,1)S(1)}, bf16[32,64]{1,0:T(8,128)(2,1)S(1)}, u32[]{:S(2)}, u32[]{:S(2)}) collective-permute-start(bf16[32,64]{1,0:T(8,128)(2,1)S(1)} %fusion.22), channel_id=1, source_target_pairs={{0,2},{1,3},{2,0},{3,1},{4,6},{5,7},{6,4},{7,5},{8,10},{9,11},{10,... | collective-permute-start | bytes 12296 | tf_op jit(solution)/shard_map/ppermute | solution.py:23
  161.8 3.7 %collective-permute-start.15 = (bf16[32,64]{1,0:T(8,128)(2,1)S(1)}, bf16[32,64]{1,0:T(8,128)(2,1)S(1)}, u32[]{:S(2)}, u32[]{:S(2)}) collective-permute-start(bf16[32,64]{1,0:T(8,128)(2,1)S(1)} %fusion.24), channel_id=1, source_target_pairs={{0,4},{1,5},{2,6},{3,7},{4,0},{5,1},{6,2},{7,3},{8,12},{9,13},{10,... | collective-permute-start | bytes 12296 | tf_op jit(solution)/shard_map/ppermute | solution.py:23
  166.3 3.7 %collective-permute-start.16 = (bf16[32,64]{1,0:T(8,128)(2,1)S(1)}, bf16[32,64]{1,0:T(8,128)(2,1)S(1)}, u32[]{:S(2)}, u32[]{:S(2)}) collective-permute-start(bf16[32,64]{1,0:T(8,128)(2,1)S(1)} %fusion.26), channel_id=1, source_target_pairs={{0,8},{1,9},{2,10},{3,11},{4,12},{5,13},{6,14},{7,15},{8,0},{9,1},... | collective-permute-start | bytes 12296 | tf_op jit(solution)/shard_map/ppermute | solution.py:23
  170.8 11.3 %collective-permute-start.17 = (bf16[32,64]{1,0:T(8,128)(2,1)S(1)}, bf16[32,64]{1,0:T(8,128)(2,1)S(1)}, u32[]{:S(2)}, u32[]{:S(2)}) collective-permute-start(bf16[32,64]{1,0:T(8,128)(2,1)S(1)} %fusion.28), channel_id=1, source_target_pairs={{0,16},{1,17},{2,18},{3,19},{4,20},{5,21},{6,22},{7,23},{8,24},{9,... | collective-permute-start | bytes 12296 | tf_op jit(solution)/shard_map/ppermute | solution.py:23
  171.6 15.3 %collective-permute-start.12 = (bf16[16,32,64]{2,1,0:T(8,128)(2,1)S(1)}, bf16[16,32,64]{2,1,0:T(8,128)(2,1)S(1)}, u32[]{:S(2)}, u32[]{:S(2)}) collective-permute-start(bf16[16,32,64]{2,1,0:T(8,128)(2,1)S(1)} %convolution_convert_fusion), channel_id=1, source_target_pairs={{1,0},{2,1},{3,2},{4,3},{5,4},{6,5},{7,6},{8,7},{9,8},{10,9},{11,1... | collective-permute-start | bytes 196616 | tf_op jit(solution)/shard_map/ppermute | solution.py:17
  172.9 14.6 %collective-permute-start.11 = (bf16[16,32,64]{2,1,0:T(8,128)(2,1)S(1)}, bf16[16,32,64]{2,1,0:T(8,128)(2,1)}, u32[]{:S(2)}, u32[]{:S(2)}) collective-permute-start(bf16[16,32,64]{2,1,0:T(8,128)(2,1)S(1)} %convolution_convert_fusion), channel_id=1, source_target_pairs={{0,1},{1,2},{2,3},{3,4},{4,5},{5,6},{6,7},{7,8},{8,9},{9,10},{10,1... | collective-permute-start | bytes 196616 | tf_op jit(solution)/shard_map/ppermute | solution.py:16
  176.6 18.5 %collective-permute-start.10 = (bf16[16,32,256]{2,1,0:T(8,128)(2,1)}, bf16[16,32,256]{2,1,0:T(8,128)(2,1)}, u32[]{:S(2)}, u32[]{:S(2)}) collective-permute-start(bf16[16,32,256]{2,1,0:T(8,128)(2,1)} %get-tuple-element.10), channel_id=1, source_target_pairs={{1,0},{2,1},{3,2},{4,3},{5,4},{6,5},{7,6},{8,7},{9,8},{10,9},{11,1... | collective-permute-start | bytes 786440 | tf_op jit(solution)/shard_map/ppermute | solution.py:17
  177.9 17.2 %collective-permute-start.9 = (bf16[16,32,256]{2,1,0:T(8,128)(2,1)}, bf16[16,32,256]{2,1,0:T(8,128)(2,1)}, u32[]{:S(2)}, u32[]{:S(2)}) collective-permute-start(bf16[16,32,256]{2,1,0:T(8,128)(2,1)} %get-tuple-element.10), channel_id=1, source_target_pairs={{0,1},{1,2},{2,3},{3,4},{4,5},{5,6},{6,7},{7,8},{8,9},{9,10},{10,1... | collective-permute-start | bytes 786440 | tf_op jit(solution)/shard_map/ppermute | solution.py:16
  186.9 0.6 copy-start.6
  190.4 2.4 copy-start.4
  192.9 3.4 %copy-start.8 = (s32[1024]{0:T(1024)S(1)}, s32[1024]{0:T(1024)}, u32[]{:S(2)}) copy-start(s32[1024]{0:T(1024)} %pad_clamp_fusion.1) | copy-start | bytes 12292
  195.1 3.1 %copy-start.11 = (f32[16]{0:T(128)S(1)}, f32[16]{0:T(128)}, u32[]{:S(2)}) copy-start(f32[16]{0:T(128)} %copy-done.9) | copy-start | bytes 196
  198.2 8.4 %copy-start.14 = (f32[32]{0:T(128)S(1)}, f32[32]{0:T(128)}, u32[]{:S(2)}) copy-start(f32[32]{0:T(128)} %copy-done.13) | copy-start | bytes 388
  198.2 49.7 %copy-start.2 = (f32[16,32,256]{2,1,0:T(8,128)S(1)}, f32[16,32,256]{2,1,0:T(8,128)}, u32[]{:S(2)}) copy-start(f32[16,32,256]{2,1,0:T(8,128)} %get-tuple-element.11) | copy-start | bytes 1572868
  206.6 43.3 %copy-start.17 = (f32[1,32]{1,0:T(1,128)S(1)}, f32[1,32]{1,0:T(1,128)}, u32[]{:S(2)}) copy-start(f32[1,32]{1,0:T(1,128)} %get-tuple-element.17) | copy-start | bytes 388
  206.7 43.3 %copy-start.18 = (f32[1,32]{1,0:T(1,128)S(1)}, f32[1,32]{1,0:T(1,128)}, u32[]{:S(2)}) copy-start(f32[1,32]{1,0:T(1,128)} %get-tuple-element.19) | copy-start | bytes 388
  206.7 43.3 %copy-start.19 = (f32[1,32]{1,0:T(1,128)S(1)}, f32[1,32]{1,0:T(1,128)}, u32[]{:S(2)}) copy-start(f32[1,32]{1,0:T(1,128)} %get-tuple-element.20) | copy-start | bytes 388
where the time goes:
time: 255 us; the launch traced here: 251 us
  blocking collectives  124 us (49%)
  matrix products  53.3 us (21%)
  starting transfers between devices  36.8 us (14%)
  other arithmetic  15.8 us (6%)
  local copies, waits for them, and re-layouts  10.7 us (4%)
  waiting for transfers between devices  8.7 us (3%)
    psum x2, blocking collectives, joint_totals(): return lax.psum(stacked, 'leaf')  82.4 us
    psum x1, blocking collectives, global_norm(): return jnp.sqrt(lax.psum(column_sums(field, field), 'leaf') + epsilon)  42 us
    dot_general x2, matrix products, apply_operator(): jnp.einsum('inrp,inpq->irq', columns, near_tile, preferred_element_type=j...  16.6 us
    ppermute x4, starting transfers between devices, with_halo(): before = lax.ppermute(last, axis, up)  16.1 us
    ppermute x10, starting transfers between devices, swapped(): lax.ppermute(array, axis, [(i, i ^ 1 << stride) for i in range(lax.axis_s...  15.5 us
    ppermute x10, waiting for transfers between devices, swapped(): lax.ppermute(array, axis, [(i, i ^ 1 << stride) for i in range(lax.axis_s...  8.68 us
    dot_general x9, matrix products, apply_operator(): jnp.einsum('rj,kj->rk', downward, tree_up[own_node], preferred_element_ty...  8.63 us
    dot_general x8, matrix products, apply_operator(): jnp.dot(sibling, tree_up[other_node], preferred_element_type=jnp.float32)  6.73 us
  transfers between devices with their start and end apart: 18, of which 8 were waited for; matrix products, arithmetic and copies ran while one was open for 15% of the time, Pallas kernels for 0%

commit v1 on v0

v1 whole, which is shorter than its diff:
```python
import functools
import jax
import jax.numpy as jnp
from jax import lax
from jax.experimental import pallas as pl
from jax.experimental.pallas import tpu as pltpu
from jax.sharding import PartitionSpec as P

epsilon = 1e-06
GROUP = 8
F32 = jnp.float32
BF16 = jnp.bfloat16


def dot(a, b):
    return jnp.dot(a, b, preferred_element_type=F32)


def dot_nt(a, b):
    return lax.dot_general(a, b, (((1,), (1,)), ((), ())), preferred_element_type=F32)


def to_columns(rows):
    return jnp.transpose(jnp.concatenate([rows] * 16, axis=0))


def kernel(
    n,
    live_ref,
    near_idx,
    far_idx,
    rhs_hbm,
    near_hbm,
    far_hbm,
    basis_hbm,
    transfer_hbm,
    up_hbm,
    couple_hbm,
    out_ref,
    hess_ref,
    rhs,
    near_t,
    far_t,
    basis,
    transfer,
    up,
    couple,
    own_0,
    own_1,
    full_0,
    full_1,
    mom_0,
    mom_1,
    local,
    w1,
    w2,
    weight_a,
    weight_b,
    twice,
    gat_a,
    gat_b,
    red_a,
    red_b,
    load_sem,
    near_sem,
    halo_send,
    halo_recv,
    a_send,
    a_recv,
    b_send,
    b_recv,
    ra_send,
    ra_recv,
    rb_send,
    rb_recv,
):
    slots, cols, points = rhs.shape
    own, full, mom = (own_0, own_1), (full_0, full_1), (mom_0, mom_1)
    rank = basis.shape[1]
    reach = (full_0.shape[0] - slots) // 2
    near_count = near_idx.shape[1]
    far_count = far_idx.shape[1]
    groups = n // GROUP
    levels = n.bit_length() - 1
    low = GROUP.bit_length() - 1
    me = lax.axis_index("leaf")
    j = me % GROUP
    base = me - j
    q = me // GROUP

    def load(hbm, vmem, k):
        return pltpu.make_async_copy(hbm, vmem, load_sem.at[k])

    loads = [
        load(rhs_hbm, rhs, 0),
        load(basis_hbm, basis, 1),
        load(transfer_hbm, transfer, 2),
        load(up_hbm, up, 3),
        load(couple_hbm, couple, 4),
        load(far_hbm, far_t, 5),
    ]
    for c in loads[:5]:
        c.start()

    def near_load(i):
        return pltpu.make_async_copy(near_hbm.at[i], near_t.at[i], near_sem.at[i])

    def start_near(i, carry):
        near_load(i).start()
        return carry

    lax.fori_loop(0, slots, start_near, 0)
    loads[5].start()

    for a in range(2):
        full[a][0:reach] = jnp.zeros((reach, cols, points), BF16)
        full[a][reach + slots : slots + 2 * reach] = jnp.zeros((reach, cols, points), BF16)
        mom[a][0:slots] = jnp.zeros((slots, cols, 2 * rank), BF16)
        mom[a][2 * slots : 3 * slots] = jnp.zeros((slots, cols, 2 * rank), BF16)

    barrier = pltpu.get_barrier_semaphore()

    def greet(dev):
        pl.semaphore_signal(barrier, inc=1, device_id=(dev,), device_id_type=pl.DeviceIdType.MESH)

    for k in range(1, GROUP):
        greet(base + (j + k) % GROUP)
    for k in range(1, groups):
        greet(((q + k) % groups) * GROUP + j)
    greet((me + 1) % n)
    greet((me + n - 1) % n)

    def remote(src, dst, send_sem, recv_sem, dev):
        return pltpu.make_async_remote_copy(
            src_ref=src,
            dst_ref=dst,
            send_sem=send_sem,
            recv_sem=recv_sem,
            device_id=(dev,),
            device_id_type=pl.DeviceIdType.MESH,
        )

    def copies_a(buf, s, r):
        return [
            remote(buf.at[j], buf.at[j], s.at[k - 1], r.at[k - 1], base + (j + k) % GROUP)
            for k in range(1, GROUP)
        ]

    def copies_b(buf, s, r):
        return [
            remote(buf.at[q], buf.at[q], s.at[k - 1], r.at[k - 1], ((q + k) % groups) * GROUP + j)
            for k in range(1, groups)
        ]

    def arrive_a(buf, s, r):
        for k in range(1, GROUP):
            src = (j + GROUP - k) % GROUP
            remote(buf.at[src], buf.at[src], s.at[k - 1], r.at[k - 1], base + src).wait_recv()

    def arrive_b(buf, s, r):
        for k in range(1, groups):
            src = (q + groups - k) % groups
            remote(
                buf.at[src], buf.at[src], s.at[k - 1], r.at[k - 1], src * GROUP + j
            ).wait_recv()

    def halo(a, kind):
        if kind == 0:
            up_src, up_dst = own[a].at[slots - reach : slots], full[a].at[0:reach]
            dn_src = own[a].at[0:reach]
            dn_dst = full[a].at[reach + slots : slots + 2 * reach]
        else:
            up_src, up_dst = mom[a].at[slots : 2 * slots], mom[a].at[0:slots]
            dn_src, dn_dst = mom[a].at[slots : 2 * slots], mom[a].at[2 * slots : 3 * slots]
        to_up = remote(up_src, up_dst, halo_send.at[a, kind, 0], halo_recv.at[a, kind, 0], (me + 1) % n)
        to_dn = remote(
            dn_src, dn_dst, halo_send.at[a, kind, 1], halo_recv.at[a, kind, 1], (me + n - 1) % n
        )
        return to_up, to_dn

    def halo_start(a, kind):
        to_up, to_dn = halo(a, kind)
        pl.when(me < n - 1)(to_up.start)
        pl.when(me > 0)(to_dn.start)

    def halo_arrive(a, kind):
        to_up, to_dn = halo(a, kind)
        pl.when(me > 0)(to_up.wait_recv)
        pl.when(me < n - 1)(to_dn.wait_recv)

    def halo_finish(a, kind):
        to_up, to_dn = halo(a, kind)
        pl.when(me < n - 1)(to_up.wait_send)
        pl.when(me > 0)(to_dn.wait_send)

    lane = lax.broadcasted_iota(jnp.int32, (cols, 2 * rank), 1)
    left_half = lane < rank

    def pair(x, y):
        return jnp.where(left_half, x, y)

    def halved(dup, parity):
        keep = (lane // rank) == parity
        return jnp.where(keep, dup, 0.0).astype(BF16)

    def moment_loop(a):
        def step(t, carry):
            i0 = t * 4
            got = []
            for u in range(4):
                b = basis[i0 + u]
                got.append(dot_nt(own[a][i0 + u], jnp.concatenate([b, b], axis=0)).astype(BF16))
            for u in range(4):
                mom[a][slots + i0 + u] = got[u]
            return carry

        lax.fori_loop(0, slots // 4, step, 0)

    def box_start(a):
        flat = jnp.concatenate(
            [pair(mom[a][slots + 2 * p], mom[a][slots + 2 * p + 1]) for p in range(slots // 2)],
            axis=1,
        )
        gat_a[a, j] = halved(dot(flat, twice[...]), j % 2)
        for c in copies_a(gat_a.at[a], a_send.at[a], a_recv.at[a]):
            c.start()

    def near_rows(a, rows, wait_tiles, src, shift):
        got = []
        first = me * slots - shift
        last = src[a].shape[0] - 1
        for i in rows:
            if wait_tiles:
                near_load(i).wait()
            v = jnp.concatenate(
                [src[a][jnp.clip(near_idx[i, k] - first, 0, last)] for k in range(near_count)], axis=1
            )
            got.append(dot(v, near_t[i].reshape(near_count * points, points)))
        for i, g in zip(rows, got):
            w2[i] = g

    def near_inner(a, lo, hi):
        def step(t, carry):
            i0 = lo + t * 4
            near_rows(a, [i0 + u for u in range(4)], a == 0, own, 0)
            return carry

        lax.fori_loop(0, (hi - lo) // 4, step, 0)

    def group_round(a):
        arrive_a(gat_a.at[a], a_send.at[a], a_recv.at[a])
        cat = jnp.concatenate(
            [gat_a[a, 2 * p] + gat_a[a, 2 * p + 1] for p in range(GROUP // 2)], axis=1
        )
        got = dot(cat, weight_a[...])
        gat_b[a, q] = halved(got[:, 2 * rank : 4 * rank], q % 2)
        for c in copies_b(gat_b.at[a], b_send.at[a], b_recv.at[a]):
            c.start()
        return got[:, : 2 * rank]

    def cross_round(a, part):
        arrive_b(gat_b.at[a], b_send.at[a], b_recv.at[a])
        cat = jnp.concatenate(
            [gat_b[a, 2 * p] + gat_b[a, 2 * p + 1] for p in range(groups // 2)], axis=1
        )
        total = part + dot(cat, weight_b[...])[:, : 2 * rank]
        return total[:, :rank].astype(BF16)

    def far_loop(a, down):
        first = me * slots - slots

        def source(i, f):
            return mom[a][jnp.clip(far_idx[i, f] - first, 0, 3 * slots - 1)]

        def step(t, carry):
            got = []
            for u in range(4):
                i = t * 4 + u
                v = jnp.concatenate(
                    [
                        pair(source(i, 2 * p), source(i, 2 * p + 1))
                        for p in range(far_count // 2)
                    ],
                    axis=1,
                )
                tr = transfer[pl.ds(pl.multiple_of(i * rank, rank), rank), :]
                got.append((dot(v, far_t[i]) + dot_nt(down, tr)).astype(BF16))
            for u in range(4):
                local[t * 4 + u] = got[u]
            return carry

        lax.fori_loop(0, slots // 4, step, 0)

    def spread(i):
        mask = live_ref[i].astype(F32)
        return (w2[i] + dot(local[i], basis[i])) * mask

    def fold(x):
        return x[:, : points // 2] + x[:, points // 2 :]

    def pack(parts):
        wide = lax.broadcasted_iota(jnp.int32, (cols, 128), 1)
        total = jnp.zeros((cols, 128), F32)
        for k, p in enumerate(parts):
            total = total + jnp.where(wide == k, jnp.sum(p, axis=1, keepdims=True), 0.0)
        padded = jnp.concatenate([total, jnp.zeros((128 - cols, 128), F32)], axis=0)
        return jnp.transpose(padded)[:8]

    def reduce_first(t, rows):
        red_a[t, j] = rows
        for c in copies_a(red_a.at[t], ra_send.at[t], ra_recv.at[t]):
            c.start()

    def reduce_second(t):
        arrive_a(red_a.at[t], ra_send.at[t], ra_recv.at[t])
        total = red_a[t, 0]
        for k in range(1, GROUP):
            total = total + red_a[t, k]
        red_b[t, q] = total
        for c in copies_b(red_b.at[t], rb_send.at[t], rb_recv.at[t]):
            c.start()

    def reduce_third(t):
        arrive_b(red_b.at[t], rb_send.at[t], rb_recv.at[t])
        total = red_b[t, 0]
        for k in range(1, groups):
            total = total + red_b[t, k]
        return total

    loads[0].wait()

    def start_step(i, acc):
        s = rhs[i] * live_ref[i].astype(F32)
        rhs[i] = s
        v = s.astype(BF16)
        own[0][i] = v
        full[0][reach + i] = v
        return acc + fold(s * s)

    norm_part = lax.fori_loop(0, slots, start_step, jnp.zeros((cols, points // 2), F32))
    pl.semaphore_wait(barrier, GROUP - 1 + groups - 1 + 2)
    halo_start(0, 0)
    loads[1].wait()
    moment_loop(0)
    halo_start(0, 1)

    rowi = lax.broadcasted_iota(jnp.int32, (rank, 2 * rank), 0)
    coli = lax.broadcasted_iota(jnp.int32, (rank, 2 * rank), 1)
    eye_twice = jnp.where(rowi == coli % rank, 1.0, 0.0).astype(BF16)
    loads[2].wait()
    twice[...] = dot(transfer[...], eye_twice).astype(BF16)
    box_start(0)
    reduce_first(0, pack([norm_part]))

    loads[3].wait()
    loads[4].wait()

    def node_row(level, node):
        return pl.multiple_of((2 * n - 2 * (n >> level) + node) * rank, rank)

    def node_up(level, node, count):
        return up[pl.ds(node_row(level, node), count * rank), :]

    path = None
    couples = []
    for level in range(levels):
        c = couple[pl.ds(node_row(level, me >> level), rank), :]
        if path is None:
            r4 = lax.broadcasted_iota(jnp.int32, (4 * rank, rank), 0)
            c4 = lax.broadcasted_iota(jnp.int32, (4 * rank, rank), 1)
            path_pad = jnp.where(r4 == c4, 1.0, 0.0).astype(BF16)
        else:
            path_pad = jnp.concatenate([path, jnp.zeros((3 * rank, rank), BF16)], axis=0)
        couples.append(dot_nt(c, path_pad))
        if level < levels - 1:
            u = node_up(level, me >> level, 1)
            path = u if path is None else dot(path, u).astype(BF16)

    def own_sibling(level, node):
        sibling = (me >> level) ^ 1
        f0 = jnp.where(sibling == node, 1.0, 0.0).astype(F32)
        f1 = jnp.where(sibling == node + 1, 1.0, 0.0).astype(F32)
        return jnp.concatenate([couples[level] * f0, couples[level] * f1], axis=0)

    wide_r = lax.broadcasted_iota(jnp.int32, (rank, 4 * rank), 0)
    wide_c = lax.broadcasted_iota(jnp.int32, (rank, 4 * rank), 1)
    root = jnp.where((wide_c >= 2 * rank) & (wide_r == wide_c % rank), 1.0, 0.0).astype(BF16)
    nodes = [root]
    for level in reversed(range(low)):
        below = []
        for m, x in enumerate(nodes):
            node = (base >> level) + 2 * m
            both = (dot(node_up(level, node, 2), x) + own_sibling(level, node)).astype(BF16)
            below.extend([both[:rank], both[rank:]])
        nodes = below
    for k, x in enumerate(nodes):
        weight_a[k * rank : (k + 1) * rank, :] = x
    nodes = [None]
    for level in reversed(range(low, levels)):
        below = []
        for m, x in enumerate(nodes):
            both = own_sibling(level, 2 * m)
            if x is not None:
                both = both + dot(node_up(level, 2 * m, 2), x)
            both = both.astype(BF16)
            below.extend([both[:rank], both[rank:]])
        nodes = below
    for k, x in enumerate(nodes):
        weight_b[k * rank : (k + 1) * rank, :] = x

    def operator_middle(a):
        near_inner(a, reach, reach + 4)
        part = group_round(a)
        if a == 0:
            reduce_second(0)
        near_inner(a, reach + 4, slots - reach)
        halo_arrive(a, 0)
        near_rows(a, [0, 1, slots - 2, slots - 1], a == 0, full, reach)
        down = cross_round(a, part)
        if a == 0:
            loads[5].wait()
        halo_arrive(a, 1)
        far_loop(a, down)

    operator_middle(0)
    norm_row = jnp.sqrt(reduce_third(0) + epsilon)
    inv_norm = to_columns(1.0 / norm_row)[:cols, 0:1]
    own_square = red_b[0, 0]
    for k in range(1, groups):
        own_square = own_square + red_b[0, k]

    def image_step(t, carry):
        got = [spread(t * 4 + u) * inv_norm for u in range(4)]
        for u in range(4):
            i = t * 4 + u
            v = got[u].astype(BF16)
            w1[i] = got[u]
            own[1][i] = v
            full[1][reach + i] = v
        return carry

    lax.fori_loop(0, slots // 4, image_step, 0)
    halo_start(1, 0)
    moment_loop(1)
    halo_start(1, 1)
    box_start(1)
    operator_middle(1)

    def gram_step(t, accs):
        got = [spread(t * 4 + u) for u in range(4)]
        for u in range(4):
            i = t * 4 + u
            z = got[u]
            w2[i] = z
            b = rhs[i] * inv_norm
            w = w1[i]
            accs = (
                accs[0] + fold(b * w),
                accs[1] + fold(w * w),
                accs[2] + fold(b * z),
                accs[3] + fold(w * z),
                accs[4] + fold(z * z),
            )
        return accs

    zero = jnp.zeros((cols, points // 2), F32)
    accs = lax.fori_loop(0, slots // 4, gram_step, (zero,) * 5)
    reduce_first(1, pack(accs))
    reduce_second(1)
    sums = reduce_third(1)

    norm = norm_row[0:1]
    unit = own_square[0:1] / (norm * norm)
    h, e, f, g, k2 = (sums[k : k + 1] for k in range(5))
    first_square = jnp.maximum(e - 2.0 * h * h + h * h * unit, 0.0)
    length = jnp.sqrt(first_square + epsilon)
    inv_l = 1.0 / length
    cross = (f - h * h) * inv_l
    inner = (g - h * e - h * f + h * h * h) * inv_l * inv_l
    image_square = (k2 - 2.0 * h * g + h * h * e) * inv_l * inv_l
    second_square = (
        image_square
        - 2.0 * cross * cross
        - 2.0 * inner * inner
        + cross * cross * unit
        + inner * inner * first_square * inv_l * inv_l
        + 2.0 * cross * inner * (h - h * unit) * inv_l
    )
    second = jnp.sqrt(jnp.maximum(second_square, 0.0) + epsilon)
    inv_s = 1.0 / second
    alpha = inv_l * inv_s
    beta = -(h + inner) * alpha
    gamma = (inner * h * inv_l - cross) * inv_s / norm
    blank = jnp.zeros((1, 128), F32)
    hess = jnp.concatenate([norm, h, length, cross, inner, second, blank, blank], axis=0)
    hess_ref[...] = hess[:6, :cols]
    coef = to_columns(jnp.concatenate([alpha, beta, gamma] + [blank] * 5, axis=0))
    ca, cb, cg = (coef[:cols, k : k + 1] for k in range(3))

    def out_step(i, carry):
        out_ref[i] = ca * w2[i] + cb * w1[i] + cg * rhs[i]
        return carry

    lax.fori_loop(0, slots, out_step, 0)

    for a in range(2):
        for c in copies_a(gat_a.at[a], a_send.at[a], a_recv.at[a]):
            c.wait_send()
        for c in copies_b(gat_b.at[a], b_send.at[a], b_recv.at[a]):
            c.wait_send()
        for c in copies_a(red_a.at[a], ra_send.at[a], ra_recv.at[a]):
            c.wait_send()
        for c in copies_b(red_b.at[a], rb_send.at[a], rb_recv.at[a]):
            c.wait_send()
        halo_finish(a, 0)
        halo_finish(a, 1)


def on_device(
    right_hand,
    leaf_live,
    near_index,
    near_tile,
    far_index,
    far_couple,
    leaf_basis,
    leaf_transfer,
    tree_up,
    tree_couple,
):
    n = lax.axis_size("leaf")
    slots, cols, points = right_hand.shape
    rank = leaf_basis.shape[1]
    far_count = far_index.shape[1]
    nodes = tree_up.shape[0]
    reach = 2
    groups = n // GROUP
    far_flat = far_couple.reshape(slots, far_count * rank, rank)
    transfer_flat = leaf_transfer.reshape(slots * rank, rank)
    up_flat = tree_up.reshape(nodes * rank, rank)
    couple_flat = tree_couple.reshape(nodes * rank, rank)
    smem = pl.BlockSpec(memory_space=pltpu.SMEM)
    anywhere = pl.BlockSpec(memory_space=pl.ANY)
    vmem = pl.BlockSpec(memory_space=pltpu.VMEM)
    dma = pltpu.SemaphoreType.DMA
    return pl.pallas_call(
        functools.partial(kernel, n),
        out_shape=(
            jax.ShapeDtypeStruct((slots, cols, points), F32),
            jax.ShapeDtypeStruct((6, cols), F32),
        ),
        in_specs=[smem] * 3 + [anywhere] * 7,
        out_specs=(vmem, vmem),
        scratch_shapes=[
            pltpu.VMEM((slots, cols, points), F32),
            pltpu.VMEM(near_tile.shape, BF16),
            pltpu.VMEM(far_flat.shape, BF16),
            pltpu.VMEM(leaf_basis.shape, BF16),
            pltpu.VMEM(transfer_flat.shape, BF16),
            pltpu.VMEM(up_flat.shape, BF16),
            pltpu.VMEM(couple_flat.shape, BF16),
            pltpu.VMEM((slots, cols, points), BF16),
            pltpu.VMEM((slots, cols, points), BF16),
            pltpu.VMEM((slots + 2 * reach, cols, points), BF16),
            pltpu.VMEM((slots + 2 * reach, cols, points), BF16),
            pltpu.VMEM((3 * slots, cols, 2 * rank), BF16),
            pltpu.VMEM((3 * slots, cols, 2 * rank), BF16),
            pltpu.VMEM((slots, cols, rank), BF16),
            pltpu.VMEM((slots, cols, points), F32),
            pltpu.VMEM((slots, cols, points), F32),
            pltpu.VMEM((GROUP * rank, 4 * rank), BF16),
            pltpu.VMEM((groups * rank, 4 * rank), BF16),
            pltpu.VMEM((slots * rank, 2 * rank), BF16),
            pltpu.VMEM((2, GROUP, cols, 2 * rank), BF16),
            pltpu.VMEM((2, groups, cols, 2 * rank), BF16),
            pltpu.VMEM((2, GROUP, 8, 128), F32),
            pltpu.VMEM((2, groups, 8, 128), F32),
            dma((6,)),
            dma((slots,)),
            dma((2, 2, 2)),
            dma((2, 2, 2)),
            dma((2, GROUP - 1)),
            dma((2, GROUP - 1)),
            dma((2, groups - 1)),
            dma((2, groups - 1)),
            dma((2, GROUP - 1)),
            dma((2, GROUP - 1)),
            dma((2, groups - 1)),
            dma((2, groups - 1)),
        ],
        compiler_params=pltpu.CompilerParams(
            collective_id=0, has_side_effects=True, vmem_limit_bytes=40 * 1024 * 1024
        ),
    )(
        leaf_live,
        near_index,
        far_index,
        right_hand,
        near_tile,
        far_flat,
        leaf_basis,
        transfer_flat,
        up_flat,
        couple_flat,
    )


def solution(mesh):
    placed = (
        P("leaf", None, None),
        P("leaf"),
        P("leaf", None),
        P("leaf", None, None, None),
        P("leaf", None),
        P("leaf", None, None, None),
        P("leaf", None, None),
        P("leaf", None, None),
        P(),
        P(),
    )
    return jax.shard_map(
        on_device,
        mesh=mesh,
        in_specs=placed,
        out_specs=(P("leaf", None, None), P()),
        check_vma=False,
    )
```

time: 255 us -> 53.5 us (0.21); the launches traced: 251 us -> 53 us
  blocking collectives: 124 us -> 0 us
  matrix products: 53.3 us -> 0 us
  Pallas kernels: 0 us -> 41.8 us
  starting transfers between devices: 36.8 us -> 0 us
  other arithmetic: 15.8 us -> 0 us
  waiting for transfers between devices: 8.7 us -> 0 us
    psum x3 -> x0, blocking collectives: 124 us -> none  [the longest x2 82.4 us: joint_totals(): return lax.psum(stacked, 'leaf')]
    dot_general x37 -> x0, matrix products: 53.3 us -> none  [the longest x2 16.6 us: apply_operator(): jnp.einsum('inrp,inpq->irq', columns, near_tile, preferred_element_type=j...]
    pallas_call x0 -> x1, Pallas kernels: none -> 41.8 us  [on_device(): pl.pallas_call(functools.partial(kernel, n), out_shape=(jax.ShapeDtypeStr...]
    ppermute x18 -> x0, starting transfers between devices: 36.8 us -> none  [the longest x4 16.1 us: with_halo(): before = lax.ppermute(last, axis, up)]
    unnamed x40 -> x18, local copies, waits for them, and re-layouts: 1.23 us -> 10.6 us
    ppermute x18 -> x0, waiting for transfers between devices: 8.7 us -> none  [the longest x10 8.68 us: swapped(): lax.ppermute(array, axis, [(i, i ^ 1 << stride) for i in range(lax.axis_s...]
    gather x4 -> x0, local copies, waits for them, and re-layouts: 8.5 us -> none  [the longest x2 4.94 us: apply_operator(): columns = padded[local_near]]
    concatenate x4 -> x0, other arithmetic: 5.38 us -> none  [with_halo(): array = jnp.concatenate([before, array, after], axis=dim)]
  transfers between devices with their start and end apart: 18 -> 0, of which waited for: 8 -> 0; matrix products, arithmetic and copies ran while one was open for 15% -> 0% of each run, Pallas kernels for 0% -> 0%
where the time goes in v1:
time: 53.5 us; the launch traced here: 53 us
  Pallas kernels  41.8 us (78%)
  local copies, waits for them, and re-layouts  10.6 us (20%)
  between operations  0.65 us (1%)
    pallas_call x1, Pallas kernels, on_device(): pl.pallas_call(functools.partial(kernel, n), out_shape=(jax.ShapeDtypeStr...  41.8 us
    unnamed x18, local copies, waits for them, and re-layouts  10.6 us

profile of v1, /device:TPU:0, one launch (start us, length us, event | category | flops | bytes accessed | tf_op | source)
XLA Modules:
  0.0 53.0 jit_solution(15787502561741715377)
XLA Ops:
  0.6 0.8 %copy.12.near_idx = s32[16,6]{1,0:T(8,128)S(1)} copy(s32[16,6]{0,1:T(8,128)} %param.12) | data formatting | bytes 768 | tf_op args[2]
  1.4 0.8 %copy.13.far_idx = s32[16,8]{1,0:T(8,128)S(1)} copy(s32[16,8]{0,1:T(8,128)} %param.14) | data formatting | bytes 1024 | tf_op args[4]
  2.2 0.0 copy-start
  2.2 1.6 %copy-done = bf16[16,8,64,64]{3,2,1,0:T(8,128)(2,1)S(1)} copy-done((bf16[16,8,64,64]{3,2,1,0:T(8,128)(2,1)S(1)}, bf16[16,8,64,64]{3,2,1,0:T(8,128)(2,1)}, u32[]{:S(2)}) %copy-start) | copy-done | bytes 1048600
  3.7 0.0 copy-start.1
  3.7 1.2 %copy-done.1 = bf16[62,64,64]{2,1,0:T(8,128)(2,1)S(1)} copy-done((bf16[62,64,64]{2,1,0:T(8,128)(2,1)S(1)}, bf16[62,64,64]{2,1,0:T(8,128)(2,1)}, u32[]{:S(2)}) %copy-start.1) | copy-done | bytes 507928
  5.0 0.0 copy-start.2
  5.0 1.2 %copy-done.2 = bf16[62,64,64]{2,1,0:T(8,128)(2,1)S(1)} copy-done((bf16[62,64,64]{2,1,0:T(8,128)(2,1)S(1)}, bf16[62,64,64]{2,1,0:T(8,128)(2,1)}, u32[]{:S(2)}) %copy-start.2) | copy-done | bytes 507928
  6.2 0.0 copy-start.3
  6.2 1.0 %copy-done.3 = f32[16,32,256]{2,1,0:T(8,128)S(1)} copy-done((f32[16,32,256]{2,1,0:T(8,128)S(1)}, f32[16,32,256]{2,1,0:T(8,128)}, u32[]{:S(2)}) %copy-start.3) | copy-done | bytes 524312
  7.2 0.0 copy-start.4
  7.2 1.0 %copy-done.4 = bf16[16,64,256]{2,1,0:T(8,128)(2,1)S(1)} copy-done((bf16[16,64,256]{2,1,0:T(8,128)(2,1)S(1)}, bf16[16,64,256]{2,1,0:T(8,128)(2,1)}, u32[]{:S(2)}) %copy-start.4) | copy-done | bytes 524312
  8.3 0.0 copy-start.5
  8.3 0.9 %copy-done.5 = bf16[16,64,64]{2,1,0:T(8,128)(2,1)S(1)} copy-done((bf16[16,64,64]{2,1,0:T(8,128)(2,1)S(1)}, bf16[16,64,64]{2,1,0:T(8,128)(2,1)}, u32[]{:S(2)}) %copy-start.5) | copy-done | bytes 131096
  9.2 0.0 copy-start.6
  9.2 0.7 %copy-done.6 = s32[16]{0:T(128)S(1)} copy-done((s32[16]{0:T(128)S(1)}, s32[16]{0:T(128)}, u32[]{:S(2)}) %copy-start.6) | copy-done | bytes 88
  9.9 41.8 %shard_map.113 = (f32[16,32,256]{2,1,0:T(8,128)S(1)}, f32[6,32]{1,0:T(8,128)S(1)}) custom-call(s32[16]{0:T(128)S(1)} %copy-done.6, s32[16,6]{1,0:T(8,128)S(1)} %copy.12.near_idx, s32[16,8]{1,0:T(8,128)S(1)} %copy.13.far_idx, f32[16,32,256]{2,1,0:T(8,128)S(1)} %copy-done.3, bf16[16,6,256,256]{3,2,1,0:T(8,128)(2,1)} %near_hbm.1, ...), custom_call_target="tpu_custom_call" | custom-call | tf_op jit(solution)/shard_map/pallas_call | solution.py:546
  51.6 0.8 %copy.16 = f32[16,32,256]{2,1,0:T(8,128)} copy(f32[16,32,256]{2,1,0:T(8,128)S(1)} %get-tuple-element.4) | data formatting | bytes 1048576
  52.4 0.6 %copy.17 = f32[6,32]{1,0:T(8,128)} copy(f32[6,32]{1,0:T(8,128)S(1)} %get-tuple-element.5) | data formatting | bytes 1536
Async XLA Ops:
  2.2 1.6 %copy-start = (bf16[16,8,64,64]{3,2,1,0:T(8,128)(2,1)S(1)}, bf16[16,8,64,64]{3,2,1,0:T(8,128)(2,1)}, u32[]{:S(2)}) copy-start(bf16[16,8,64,64]{3,2,1,0:T(8,128)(2,1)} %param.15) | copy-start | bytes 3145732
  3.7 1.2 %copy-start.1 = (bf16[62,64,64]{2,1,0:T(8,128)(2,1)S(1)}, bf16[62,64,64]{2,1,0:T(8,128)(2,1)}, u32[]{:S(2)}) copy-start(bf16[62,64,64]{2,1,0:T(8,128)(2,1)} %param.18) | copy-start | bytes 1523716
  5.0 1.2 %copy-start.2 = (bf16[62,64,64]{2,1,0:T(8,128)(2,1)S(1)}, bf16[62,64,64]{2,1,0:T(8,128)(2,1)}, u32[]{:S(2)}) copy-start(bf16[62,64,64]{2,1,0:T(8,128)(2,1)} %param.19) | copy-start | bytes 1523716
  6.2 1.0 %copy-start.3 = (f32[16,32,256]{2,1,0:T(8,128)S(1)}, f32[16,32,256]{2,1,0:T(8,128)}, u32[]{:S(2)}) copy-start(f32[16,32,256]{2,1,0:T(8,128)} %rhs_hbm.1) | copy-start | bytes 1572868
  7.2 1.0 %copy-start.4 = (bf16[16,64,256]{2,1,0:T(8,128)(2,1)S(1)}, bf16[16,64,256]{2,1,0:T(8,128)(2,1)}, u32[]{:S(2)}) copy-start(bf16[16,64,256]{2,1,0:T(8,128)(2,1)} %basis_hbm.1) | copy-start | bytes 1572868
  8.3 0.9 %copy-start.5 = (bf16[16,64,64]{2,1,0:T(8,128)(2,1)S(1)}, bf16[16,64,64]{2,1,0:T(8,128)(2,1)}, u32[]{:S(2)}) copy-start(bf16[16,64,64]{2,1,0:T(8,128)(2,1)} %param.17) | copy-start | bytes 393220
  9.2 0.7 %copy-start.6 = (s32[16]{0:T(128)S(1)}, s32[16]{0:T(128)}, u32[]{:S(2)}) copy-start(s32[16]{0:T(128)} %live_ref.1) | copy-start | bytes 196

commit v2 on v1

--- a/solution.py
+++ b/solution.py
@@ -78,8 +78,8 @@
     own, full, mom = (own_0, own_1), (full_0, full_1), (mom_0, mom_1)
     rank = basis.shape[1]
     reach = (full_0.shape[0] - slots) // 2
-    near_count = near_idx.shape[1]
-    far_count = far_idx.shape[1]
+    near_count = near_idx.shape[0]
+    far_count = far_idx.shape[0]
     groups = n // GROUP
     levels = n.bit_length() - 1
     low = GROUP.bit_length() - 1
@@ -205,16 +205,16 @@
 
     def moment_loop(a):
         def step(t, carry):
-            i0 = t * 4
+            i0 = t * 8
             got = []
-            for u in range(4):
+            for u in range(8):
                 b = basis[i0 + u]
                 got.append(dot_nt(own[a][i0 + u], jnp.concatenate([b, b], axis=0)).astype(BF16))
-            for u in range(4):
+            for u in range(8):
                 mom[a][slots + i0 + u] = got[u]
             return carry
 
-        lax.fori_loop(0, slots // 4, step, 0)
+        lax.fori_loop(0, slots // 8, step, 0)
 
     def box_start(a):
         flat = jnp.concatenate(
@@ -233,7 +233,7 @@
             if wait_tiles:
                 near_load(i).wait()
             v = jnp.concatenate(
-                [src[a][jnp.clip(near_idx[i, k] - first, 0, last)] for k in range(near_count)], axis=1
+                [src[a][jnp.clip(near_idx[k, i] - first, 0, last)] for k in range(near_count)], axis=1
             )
             got.append(dot(v, near_t[i].reshape(near_count * points, points)))
         for i, g in zip(rows, got):
@@ -270,12 +270,12 @@
         first = me * slots - slots
 
         def source(i, f):
-            return mom[a][jnp.clip(far_idx[i, f] - first, 0, 3 * slots - 1)]
+            return mom[a][jnp.clip(far_idx[f, i] - first, 0, 3 * slots - 1)]
 
         def step(t, carry):
             got = []
-            for u in range(4):
-                i = t * 4 + u
+            for u in range(8):
+                i = t * 8 + u
                 v = jnp.concatenate(
                     [
                         pair(source(i, 2 * p), source(i, 2 * p + 1))
@@ -285,11 +285,11 @@
                 )
                 tr = transfer[pl.ds(pl.multiple_of(i * rank, rank), rank), :]
                 got.append((dot(v, far_t[i]) + dot_nt(down, tr)).astype(BF16))
-            for u in range(4):
-                local[t * 4 + u] = got[u]
+            for u in range(8):
+                local[t * 8 + u] = got[u]
             return carry
 
-        lax.fori_loop(0, slots // 4, step, 0)
+        lax.fori_loop(0, slots // 8, step, 0)
 
     def spread(i):
         mask = live_ref[i].astype(F32)
@@ -540,7 +540,7 @@
     up_flat = tree_up.reshape(nodes * rank, rank)
     couple_flat = tree_couple.reshape(nodes * rank, rank)
     smem = pl.BlockSpec(memory_space=pltpu.SMEM)
-    anywhere = pl.BlockSpec(memory_space=pl.ANY)
+    anywhere = pl.BlockSpec(memory_space=pltpu.HBM)
     vmem = pl.BlockSpec(memory_space=pltpu.VMEM)
     dma = pltpu.SemaphoreType.DMA
     return pl.pallas_call(
@@ -589,12 +589,12 @@
             dma((2, groups - 1)),
         ],
         compiler_params=pltpu.CompilerParams(
-            collective_id=0, has_side_effects=True, vmem_limit_bytes=40 * 1024 * 1024
+            collective_id=0, has_side_effects=True, vmem_limit_bytes=60 * 1024 * 1024
         ),
     )(
         leaf_live,
-        near_index,
-        far_index,
+        near_index.T,
+        far_index.T,
         right_hand,
         near_tile,
         far_flat,

time: 53.5 us -> 45.1 us (0.84)
  local copies, waits for them, and re-layouts: 10.6 us -> 3.15 us
  Pallas kernels: 41.8 us -> 41.1 us
    unnamed x18 -> x2, local copies, waits for them, and re-layouts: 10.6 us -> 3.15 us
    pallas_call x1, Pallas kernels: 41.8 us -> 41.1 us  [on_device(): pl.pallas_call(functools.partial(kernel, n), out_shape=(jax.ShapeDtypeStr...]
where the time goes in v2:
time: 45.1 us; the launch traced here: 44.9 us
  Pallas kernels  41.1 us (91%)
  local copies, waits for them, and re-layouts  3.15 us (7%)
  between operations  0.64 us (1%)
    pallas_call x1, Pallas kernels, on_device(): pl.pallas_call(functools.partial(kernel, n), out_shape=(jax.ShapeDtypeStr...  41.1 us
    unnamed x2, local copies, waits for them, and re-layouts  3.15 us

profile of v2, /device:TPU:0, one launch (start us, length us, event | category | flops | bytes accessed | tf_op | source)
XLA Modules:
  0.0 44.9 jit_solution(13647330140984724327)
XLA Ops:
  0.6 41.1 %shard_map.113 = (f32[16,32,256]{2,1,0:T(8,128)}, f32[6,32]{1,0:T(8,128)}) custom-call(s32[16]{0:T(128)} %live_ref.1, s32[6,16]{1,0:T(8,128)} %bitcast.10, s32[8,16]{1,0:T(8,128)} %bitcast.11, f32[16,32,256]{2,1,0:T(8,128)} %rhs_hbm.1, bf16[16,6,256,256]{3,2,1,0:T(8,128)(2,1)} %near_hbm.1, bf16[16,512,64]{2,1,0:T(8,128)(2,1)} %bitcast.6, ...), custom_call_target="tpu_custom_call" | custom-call | tf_op jit(solution)/shard_map/pallas_call | solution.py:546
  41.7 1.9 %copy.14 = f32[16,32,256]{2,1,0:T(8,128)} copy(f32[16,32,256]{2,1,0:T(8,128)} %get-tuple-element.4) | data formatting | bytes 1048576
  43.6 1.3 %copy.15 = f32[6,32]{1,0:T(8,128)} copy(f32[6,32]{1,0:T(8,128)} %get-tuple-element.5) | data formatting | bytes 1536

commit v3 on v2

--- a/solution.py
+++ b/solution.py
@@ -57,6 +57,8 @@
     weight_a,
     weight_b,
     twice,
+    basis_t,
+    spread_w,
     gat_a,
     gat_b,
     red_a,
@@ -208,13 +210,32 @@
             i0 = t * 8
             got = []
             for u in range(8):
-                b = basis[i0 + u]
-                got.append(dot_nt(own[a][i0 + u], jnp.concatenate([b, b], axis=0)).astype(BF16))
+                got.append(dot(own[a][i0 + u], basis_t[i0 + u]).astype(BF16))
             for u in range(8):
                 mom[a][slots + i0 + u] = got[u]
             return carry
 
         lax.fori_loop(0, slots // 8, step, 0)
+
+    def transpose_basis(i, carry):
+        b = basis[i]
+        basis_t[i] = jnp.transpose(jnp.concatenate([b, b], axis=0))
+        return carry
+
+    def spread_weights(t, carry):
+        got = []
+        for u in range(4):
+            i = t * 4 + u
+            tr = transfer[pl.ds(pl.multiple_of(i * rank, rank), rank), :]
+            got.append(
+                lax.dot_general(
+                    tr, basis[i], (((0,), (0,)), ((), ())), preferred_element_type=F32
+                ).astype(BF16)
+            )
+        for u in range(4):
+            spread_w[t * 4 + u, 0:rank] = basis[t * 4 + u]
+            spread_w[t * 4 + u, rank : 2 * rank] = got[u]
+        return carry
 
     def box_start(a):
         flat = jnp.concatenate(
@@ -264,9 +285,9 @@
             [gat_b[a, 2 * p] + gat_b[a, 2 * p + 1] for p in range(groups // 2)], axis=1
         )
         total = part + dot(cat, weight_b[...])[:, : 2 * rank]
-        return total[:, :rank].astype(BF16)
-
-    def far_loop(a, down):
+        return total.astype(BF16)
+
+    def far_loop(a):
         first = me * slots - slots
 
         def source(i, f):
@@ -283,17 +304,16 @@
                     ],
                     axis=1,
                 )
-                tr = transfer[pl.ds(pl.multiple_of(i * rank, rank), rank), :]
-                got.append((dot(v, far_t[i]) + dot_nt(down, tr)).astype(BF16))
+                got.append(dot(v, far_t[i]).astype(BF16))
             for u in range(8):
-                local[t * 8 + u] = got[u]
+                local[t * 8 + u, :, 0:rank] = got[u]
             return carry
 
         lax.fori_loop(0, slots // 8, step, 0)
 
-    def spread(i):
+    def spread(i, down):
         mask = live_ref[i].astype(F32)
-        return (w2[i] + dot(local[i], basis[i])) * mask
+        return (w2[i] + dot(pair(local[i], down), spread_w[i])) * mask
 
     def fold(x):
         return x[:, : points // 2] + x[:, points // 2 :]
@@ -341,6 +361,7 @@
     pl.semaphore_wait(barrier, GROUP - 1 + groups - 1 + 2)
     halo_start(0, 0)
     loads[1].wait()
+    lax.fori_loop(0, slots, transpose_basis, 0)
     moment_loop(0)
     halo_start(0, 1)
 
@@ -368,9 +389,10 @@
         if path is None:
             r4 = lax.broadcasted_iota(jnp.int32, (4 * rank, rank), 0)
             c4 = lax.broadcasted_iota(jnp.int32, (4 * rank, rank), 1)
-            path_pad = jnp.where(r4 == c4, 1.0, 0.0).astype(BF16)
+            path_pad = jnp.where((r4 % rank == c4) & (r4 < 2 * rank), 1.0, 0.0).astype(BF16)
         else:
-            path_pad = jnp.concatenate([path, jnp.zeros((3 * rank, rank), BF16)], axis=0)
+            blank_rows = jnp.zeros((2 * rank, rank), BF16)
+            path_pad = jnp.concatenate([path, path, blank_rows], axis=0)
         couples.append(dot_nt(c, path_pad))
         if level < levels - 1:
             u = node_up(level, me >> level, 1)
@@ -408,21 +430,24 @@
     for k, x in enumerate(nodes):
         weight_b[k * rank : (k + 1) * rank, :] = x
 
+    lax.fori_loop(0, slots // 4, spread_weights, 0)
+
     def operator_middle(a):
-        near_inner(a, reach, reach + 4)
+        split = reach + 4 * (a + 1)
+        near_inner(a, reach, split)
         part = group_round(a)
         if a == 0:
             reduce_second(0)
-        near_inner(a, reach + 4, slots - reach)
+        near_inner(a, split, slots - reach)
         halo_arrive(a, 0)
         near_rows(a, [0, 1, slots - 2, slots - 1], a == 0, full, reach)
-        down = cross_round(a, part)
         if a == 0:
             loads[5].wait()
         halo_arrive(a, 1)
-        far_loop(a, down)
-
-    operator_middle(0)
+        far_loop(a)
+        return cross_round(a, part)
+
+    down = operator_middle(0)
     norm_row = jnp.sqrt(reduce_third(0) + epsilon)
     inv_norm = to_columns(1.0 / norm_row)[:cols, 0:1]
     own_square = red_b[0, 0]
@@ -430,7 +455,7 @@
         own_square = own_square + red_b[0, k]
 
     def image_step(t, carry):
-        got = [spread(t * 4 + u) * inv_norm for u in range(4)]
+        got = [spread(t * 4 + u, down) * inv_norm for u in range(4)]
         for u in range(4):
             i = t * 4 + u
             v = got[u].astype(BF16)
@@ -444,10 +469,10 @@
     moment_loop(1)
     halo_start(1, 1)
     box_start(1)
-    operator_middle(1)
+    down = operator_middle(1)
 
     def gram_step(t, accs):
-        got = [spread(t * 4 + u) for u in range(4)]
+        got = [spread(t * 4 + u, down) for u in range(4)]
         for u in range(4):
             i = t * 4 + u
             z = got[u]
@@ -565,12 +590,14 @@
             pltpu.VMEM((slots + 2 * reach, cols, points), BF16),
             pltpu.VMEM((3 * slots, cols, 2 * rank), BF16),
             pltpu.VMEM((3 * slots, cols, 2 * rank), BF16),
-            pltpu.VMEM((slots, cols, rank), BF16),
+            pltpu.VMEM((slots, cols, 2 * rank), BF16),
             pltpu.VMEM((slots, cols, points), F32),
             pltpu.VMEM((slots, cols, points), F32),
             pltpu.VMEM((GROUP * rank, 4 * rank), BF16),
             pltpu.VMEM((groups * rank, 4 * rank), BF16),
             pltpu.VMEM((slots * rank, 2 * rank), BF16),
+            pltpu.VMEM((slots, points, 2 * rank), BF16),
+            pltpu.VMEM((slots, 2 * rank, points), BF16),
             pltpu.VMEM((2, GROUP, cols, 2 * rank), BF16),
             pltpu.VMEM((2, groups, cols, 2 * rank), BF16),
             pltpu.VMEM((2, GROUP, 8, 128), F32),
@@ -589,7 +616,7 @@
             dma((2, groups - 1)),
         ],
         compiler_params=pltpu.CompilerParams(
-            collective_id=0, has_side_effects=True, vmem_limit_bytes=60 * 1024 * 1024
+            collective_id=0, has_side_effects=True, vmem_limit_bytes=54016 * 1024
         ),
     )(
         leaf_live,

time: 45.1 us -> 45 us (level)
  Pallas kernels: 41.1 us -> 39.8 us
  local copies, waits for them, and re-layouts: 3.15 us -> 4.36 us
    pallas_call x1, Pallas kernels: 41.1 us -> 39.8 us  [on_device(): pl.pallas_call(functools.partial(kernel, n), out_shape=(jax.ShapeDtypeStr...]
    unnamed x2 -> x10, local copies, waits for them, and re-layouts: 3.15 us -> 4.36 us
where the time goes in v3:
time: 45 us; the launch traced here: 44.8 us
  Pallas kernels  39.8 us (88%)
  local copies, waits for them, and re-layouts  4.36 us (10%)
  between operations  0.65 us (1%)
    pallas_call x1, Pallas kernels, on_device(): pl.pallas_call(functools.partial(kernel, n), out_shape=(jax.ShapeDtypeStr...  39.8 us
    unnamed x10, local copies, waits for them, and re-layouts  4.36 us

profile of v3, /device:TPU:0, one launch (start us, length us, event | category | flops | bytes accessed | tf_op | source)
XLA Modules:
  0.0 44.8 jit_solution(7431378891308777731)
XLA Ops:
  0.6 0.0 copy-start
  0.6 0.9 %copy-done = bf16[16,64,64]{2,1,0:T(8,128)(2,1)S(1)} copy-done((bf16[16,64,64]{2,1,0:T(8,128)(2,1)S(1)}, bf16[16,64,64]{2,1,0:T(8,128)(2,1)}, u32[]{:S(2)}) %copy-start) | copy-done | bytes 131096
  1.6 0.0 copy-start.1
  1.6 0.7 %copy-done.1 = s32[16,6]{0,1:T(8,128)S(1)} copy-done((s32[16,6]{0,1:T(8,128)S(1)}, s32[16,6]{0,1:T(8,128)}, u32[]{:S(2)}) %copy-start.1) | copy-done | bytes 408
  2.3 0.0 copy-start.2
  2.3 0.7 %copy-done.2 = s32[16,8]{0,1:T(8,128)S(1)} copy-done((s32[16,8]{0,1:T(8,128)S(1)}, s32[16,8]{0,1:T(8,128)}, u32[]{:S(2)}) %copy-start.2) | copy-done | bytes 536
  3.0 0.0 copy-start.3
  3.0 0.7 %copy-done.3 = s32[16]{0:T(128)S(1)} copy-done((s32[16]{0:T(128)S(1)}, s32[16]{0:T(128)}, u32[]{:S(2)}) %copy-start.3) | copy-done | bytes 88
  3.6 39.8 %shard_map.113 = (f32[16,32,256]{2,1,0:T(8,128)S(1)}, f32[6,32]{1,0:T(8,128)S(1)}) custom-call(s32[16]{0:T(128)S(1)} %copy-done.3, s32[6,16]{1,0:T(8,128)S(1)} %bitcast.7, s32[8,16]{1,0:T(8,128)S(1)} %bitcast.8, f32[16,32,256]{2,1,0:T(8,128)} %rhs_hbm.1, bf16[16,6,256,256]{3,2,1,0:T(8,128)(2,1)} %near_hbm.1, bf16[16,512,64]{2,1,0:T(8,128)(2,1)} %bitcast.9, ...), custom_call_target="tpu_custom_call" | custom-call | tf_op jit(solution)/shard_map/pallas_call | solution.py:571
  43.4 0.8 %copy.14 = f32[16,32,256]{2,1,0:T(8,128)} copy(f32[16,32,256]{2,1,0:T(8,128)S(1)} %get-tuple-element.4) | data formatting | bytes 1048576
  44.2 0.6 %copy.15 = f32[6,32]{1,0:T(8,128)} copy(f32[6,32]{1,0:T(8,128)S(1)} %get-tuple-element.5) | data formatting | bytes 1536
Async XLA Ops:
  0.6 1.0 %copy-start = (bf16[16,64,64]{2,1,0:T(8,128)(2,1)S(1)}, bf16[16,64,64]{2,1,0:T(8,128)(2,1)}, u32[]{:S(2)}) copy-start(bf16[16,64,64]{2,1,0:T(8,128)(2,1)} %param.17) | copy-start | bytes 393220
  1.6 0.7 %copy-start.1 = (s32[16,6]{0,1:T(8,128)S(1)}, s32[16,6]{0,1:T(8,128)}, u32[]{:S(2)}) copy-start(s32[16,6]{0,1:T(8,128)} %param.12) | copy-start | bytes 1156
  2.3 0.7 %copy-start.2 = (s32[16,8]{0,1:T(8,128)S(1)}, s32[16,8]{0,1:T(8,128)}, u32[]{:S(2)}) copy-start(s32[16,8]{0,1:T(8,128)} %param.14) | copy-start | bytes 1540
  3.0 0.7 %copy-start.3 = (s32[16]{0:T(128)S(1)}, s32[16]{0:T(128)}, u32[]{:S(2)}) copy-start(s32[16]{0:T(128)} %live_ref.1) | copy-start | bytes 196

commit v4 on v3

--- a/solution.py
+++ b/solution.py
@@ -59,6 +59,7 @@
     twice,
     basis_t,
     spread_w,
+    far_four,
     gat_a,
     gat_b,
     red_a,
@@ -207,19 +208,26 @@
 
     def moment_loop(a):
         def step(t, carry):
-            i0 = t * 8
             got = []
-            for u in range(8):
-                got.append(dot(own[a][i0 + u], basis_t[i0 + u]).astype(BF16))
-            for u in range(8):
-                mom[a][slots + i0 + u] = got[u]
+            for u in range(4):
+                p = t * 4 + u
+                v = jnp.concatenate([own[a][2 * p], own[a][2 * p + 1]], axis=0)
+                got.append(dot(v, basis_t[p]).astype(BF16))
+            for u in range(4):
+                p = t * 4 + u
+                mom[a][slots + 2 * p] = got[u][:cols, : 2 * rank]
+                mom[a][slots + 2 * p + 1] = got[u][cols:, 2 * rank :]
             return carry
 
         lax.fori_loop(0, slots // 8, step, 0)
 
-    def transpose_basis(i, carry):
-        b = basis[i]
-        basis_t[i] = jnp.transpose(jnp.concatenate([b, b], axis=0))
+    def transpose_basis(p, carry):
+        b0, b1 = basis[2 * p], basis[2 * p + 1]
+        basis_t[p] = jnp.transpose(jnp.concatenate([b0, b0, b1, b1], axis=0))
+        return carry
+
+    def pack_far(t, carry):
+        far_four[t] = jnp.concatenate([far_t[t * 4 + u] for u in range(4)], axis=1)
         return carry
 
     def spread_weights(t, carry):
@@ -233,8 +241,9 @@
                 ).astype(BF16)
             )
         for u in range(4):
-            spread_w[t * 4 + u, 0:rank] = basis[t * 4 + u]
-            spread_w[t * 4 + u, rank : 2 * rank] = got[u]
+            halves = (basis[t * 4 + u], got[u])
+            spread_w[t * 4 + u, 0:rank] = halves[u % 2]
+            spread_w[t * 4 + u, rank : 2 * rank] = halves[1 - u % 2]
         return carry
 
     def box_start(a):
@@ -294,26 +303,30 @@
             return mom[a][jnp.clip(far_idx[f, i] - first, 0, 3 * slots - 1)]
 
         def step(t, carry):
-            got = []
-            for u in range(8):
-                i = t * 8 + u
-                v = jnp.concatenate(
-                    [
-                        pair(source(i, 2 * p), source(i, 2 * p + 1))
-                        for p in range(far_count // 2)
-                    ],
-                    axis=1,
+            stack = []
+            for u in range(4):
+                i = t * 4 + u
+                stack.append(
+                    jnp.concatenate(
+                        [
+                            pair(source(i, 2 * p), source(i, 2 * p + 1))
+                            for p in range(far_count // 2)
+                        ],
+                        axis=1,
+                    )
                 )
-                got.append(dot(v, far_t[i]).astype(BF16))
-            for u in range(8):
-                local[t * 8 + u, :, 0:rank] = got[u]
+            got = dot(jnp.concatenate(stack, axis=0), far_four[t]).astype(BF16)
+            for u in range(4):
+                k = (u // 2) * 2 * rank
+                local[t * 4 + u] = got[u * cols : (u + 1) * cols, k : k + 2 * rank]
             return carry
 
-        lax.fori_loop(0, slots // 8, step, 0)
-
-    def spread(i, down):
+        lax.fori_loop(0, slots // 4, step, 0)
+
+    def spread(i, odd, down):
         mask = live_ref[i].astype(F32)
-        return (w2[i] + dot(pair(local[i], down), spread_w[i])) * mask
+        both = pair(down, local[i]) if odd else pair(local[i], down)
+        return (w2[i] + dot(both, spread_w[i])) * mask
 
     def fold(x):
         return x[:, : points // 2] + x[:, points // 2 :]
@@ -361,7 +374,7 @@
     pl.semaphore_wait(barrier, GROUP - 1 + groups - 1 + 2)
     halo_start(0, 0)
     loads[1].wait()
-    lax.fori_loop(0, slots, transpose_basis, 0)
+    lax.fori_loop(0, slots // 2, transpose_basis, 0)
     moment_loop(0)
     halo_start(0, 1)
 
@@ -443,6 +456,7 @@
         near_rows(a, [0, 1, slots - 2, slots - 1], a == 0, full, reach)
         if a == 0:
             loads[5].wait()
+            lax.fori_loop(0, slots // 4, pack_far, 0)
         halo_arrive(a, 1)
         far_loop(a)
         return cross_round(a, part)
@@ -455,7 +469,7 @@
         own_square = own_square + red_b[0, k]
 
     def image_step(t, carry):
-        got = [spread(t * 4 + u, down) * inv_norm for u in range(4)]
+        got = [spread(t * 4 + u, u % 2, down) * inv_norm for u in range(4)]
         for u in range(4):
             i = t * 4 + u
             v = got[u].astype(BF16)
@@ -472,7 +486,7 @@
     down = operator_middle(1)
 
     def gram_step(t, accs):
-        got = [spread(t * 4 + u, down) for u in range(4)]
+        got = [spread(t * 4 + u, u % 2, down) for u in range(4)]
         for u in range(4):
             i = t * 4 + u
             z = got[u]
@@ -596,8 +610,9 @@
             pltpu.VMEM((GROUP * rank, 4 * rank), BF16),
             pltpu.VMEM((groups * rank, 4 * rank), BF16),
             pltpu.VMEM((slots * rank, 2 * rank), BF16),
-            pltpu.VMEM((slots, points, 2 * rank), BF16),
+            pltpu.VMEM((slots // 2, points, 4 * rank), BF16),
             pltpu.VMEM((slots, 2 * rank, points), BF16),
+            pltpu.VMEM((slots // 4, far_count * rank, 4 * rank), BF16),
             pltpu.VMEM((2, GROUP, cols, 2 * rank), BF16),
             pltpu.VMEM((2, groups, cols, 2 * rank), BF16),
             pltpu.VMEM((2, GROUP, 8, 128), F32),
@@ -616,7 +631,7 @@
             dma((2, groups - 1)),
         ],
         compiler_params=pltpu.CompilerParams(
-            collective_id=0, has_side_effects=True, vmem_limit_bytes=54016 * 1024
+            collective_id=0, has_side_effects=True, vmem_limit_bytes=60 * 1024 * 1024
         ),
     )(
         leaf_live,

time: 45 us -> 45.2 us (level)
  Pallas kernels: 39.8 us -> 41.2 us
  local copies, waits for them, and re-layouts: 4.36 us -> 3.15 us
    pallas_call x1, Pallas kernels: 39.8 us -> 41.2 us  [on_device(): pl.pallas_call(functools.partial(kernel, n), out_shape=(jax.ShapeDtypeStr...]
    unnamed x10 -> x2, local copies, waits for them, and re-layouts: 4.36 us -> 3.15 us
where the time goes in v4:
time: 45.2 us; the launch traced here: 45 us
  Pallas kernels  41.2 us (91%)
  local copies, waits for them, and re-layouts  3.15 us (7%)
  between operations  0.64 us (1%)
    pallas_call x1, Pallas kernels, on_device(): pl.pallas_call(functools.partial(kernel, n), out_shape=(jax.ShapeDtypeStr...  41.2 us
    unnamed x2, local copies, waits for them, and re-layouts  3.15 us

profile of v4, /device:TPU:0, one launch (start us, length us, event | category | flops | bytes accessed | tf_op | source)
XLA Modules:
  0.0 45.0 jit_solution(16188353309078409859)
XLA Ops:
  0.6 41.2 %shard_map.113 = (f32[16,32,256]{2,1,0:T(8,128)}, f32[6,32]{1,0:T(8,128)}) custom-call(s32[16]{0:T(128)} %live_ref.1, s32[6,16]{1,0:T(8,128)} %bitcast.10, s32[8,16]{1,0:T(8,128)} %bitcast.11, f32[16,32,256]{2,1,0:T(8,128)} %rhs_hbm.1, bf16[16,6,256,256]{3,2,1,0:T(8,128)(2,1)} %near_hbm.1, bf16[16,512,64]{2,1,0:T(8,128)(2,1)} %bitcast.6, ...), custom_call_target="tpu_custom_call" | custom-call | tf_op jit(solution)/shard_map/pallas_call | solution.py:585
  41.8 1.9 %copy.14 = f32[16,32,256]{2,1,0:T(8,128)} copy(f32[16,32,256]{2,1,0:T(8,128)} %get-tuple-element.4) | data formatting | bytes 1048576
  43.7 1.3 %copy.15 = f32[6,32]{1,0:T(8,128)} copy(f32[6,32]{1,0:T(8,128)} %get-tuple-element.5) | data formatting | bytes 1536

commit v5 on v3

--- a/solution.py
+++ b/solution.py
@@ -616,7 +616,7 @@
             dma((2, groups - 1)),
         ],
         compiler_params=pltpu.CompilerParams(
-            collective_id=0, has_side_effects=True, vmem_limit_bytes=54016 * 1024
+            collective_id=0, has_side_effects=True, vmem_limit_bytes=54400 * 1024
         ),
     )(
         leaf_live,

time: 45 us -> 45 us (level)
  no operation moved by 1% of the time
where the time goes in v5:
time: 45 us; the launch traced here: 44.8 us
  Pallas kernels  39.8 us (88%)
  local copies, waits for them, and re-layouts  4.36 us (10%)
  between operations  0.65 us (1%)
    pallas_call x1, Pallas kernels, on_device(): pl.pallas_call(functools.partial(kernel, n), out_shape=(jax.ShapeDtypeStr...  39.8 us
    unnamed x10, local copies, waits for them, and re-layouts  4.36 us

profile of v5, /device:TPU:0, one launch (start us, length us, event | category | flops | bytes accessed | tf_op | source)
XLA Modules:
  0.0 44.8 jit_solution(5399637378171816694)
XLA Ops:
  0.6 0.0 copy-start
  0.6 0.9 %copy-done = bf16[16,64,64]{2,1,0:T(8,128)(2,1)S(1)} copy-done((bf16[16,64,64]{2,1,0:T(8,128)(2,1)S(1)}, bf16[16,64,64]{2,1,0:T(8,128)(2,1)}, u32[]{:S(2)}) %copy-start) | copy-done | bytes 131096
  1.6 0.0 copy-start.1
  1.6 0.7 %copy-done.1 = s32[16,6]{0,1:T(8,128)S(1)} copy-done((s32[16,6]{0,1:T(8,128)S(1)}, s32[16,6]{0,1:T(8,128)}, u32[]{:S(2)}) %copy-start.1) | copy-done | bytes 408
  2.3 0.0 copy-start.2
  2.3 0.7 %copy-done.2 = s32[16,8]{0,1:T(8,128)S(1)} copy-done((s32[16,8]{0,1:T(8,128)S(1)}, s32[16,8]{0,1:T(8,128)}, u32[]{:S(2)}) %copy-start.2) | copy-done | bytes 536
  3.0 0.0 copy-start.3
  3.0 0.7 %copy-done.3 = s32[16]{0:T(128)S(1)} copy-done((s32[16]{0:T(128)S(1)}, s32[16]{0:T(128)}, u32[]{:S(2)}) %copy-start.3) | copy-done | bytes 88
  3.6 39.8 %shard_map.113 = (f32[16,32,256]{2,1,0:T(8,128)S(1)}, f32[6,32]{1,0:T(8,128)S(1)}) custom-call(s32[16]{0:T(128)S(1)} %copy-done.3, s32[6,16]{1,0:T(8,128)S(1)} %bitcast.7, s32[8,16]{1,0:T(8,128)S(1)} %bitcast.8, f32[16,32,256]{2,1,0:T(8,128)} %rhs_hbm.1, bf16[16,6,256,256]{3,2,1,0:T(8,128)(2,1)} %near_hbm.1, bf16[16,512,64]{2,1,0:T(8,128)(2,1)} %bitcast.9, ...), custom_call_target="tpu_custom_call" | custom-call | tf_op jit(solution)/shard_map/pallas_call | solution.py:571
  43.4 0.8 %copy.14 = f32[16,32,256]{2,1,0:T(8,128)} copy(f32[16,32,256]{2,1,0:T(8,128)S(1)} %get-tuple-element.4) | data formatting | bytes 1048576
  44.2 0.6 %copy.15 = f32[6,32]{1,0:T(8,128)} copy(f32[6,32]{1,0:T(8,128)S(1)} %get-tuple-element.5) | data formatting | bytes 1536
Async XLA Ops:
  0.6 1.0 %copy-start = (bf16[16,64,64]{2,1,0:T(8,128)(2,1)S(1)}, bf16[16,64,64]{2,1,0:T(8,128)(2,1)}, u32[]{:S(2)}) copy-start(bf16[16,64,64]{2,1,0:T(8,128)(2,1)} %param.17) | copy-start | bytes 393220
  1.6 0.7 %copy-start.1 = (s32[16,6]{0,1:T(8,128)S(1)}, s32[16,6]{0,1:T(8,128)}, u32[]{:S(2)}) copy-start(s32[16,6]{0,1:T(8,128)} %param.12) | copy-start | bytes 1156
  2.3 0.7 %copy-start.2 = (s32[16,8]{0,1:T(8,128)S(1)}, s32[16,8]{0,1:T(8,128)}, u32[]{:S(2)}) copy-start(s32[16,8]{0,1:T(8,128)} %param.14) | copy-start | bytes 1540
  3.0 0.7 %copy-start.3 = (s32[16]{0:T(128)S(1)}, s32[16]{0:T(128)}, u32[]{:S(2)}) copy-start(s32[16]{0:T(128)} %live_ref.1) | copy-start | bytes 196
